TPU v7x, 32 devices: a whole 2x2x4 slice. The times are simulated.
32 devices in a mesh: groups: 2 (over y), ra: 4 (over z), dec: 2 (over x), band: 2 (over core).
Axes of the slice: x: 2, y: 2, z: 4, core: 2. Of those that a mesh axis runs over, the one named last changes fastest.
Arguments:
- sky_maps: bfloat16 [512, 312, 256], P(('groups', 'band'), 'ra', 'dec'), parts along dimension 0, may hold values from -12 to 12
- radii: int32 [512], P(('groups', 'band')), parts along dimension 0, may hold values from 1 to 17, as said below
- valid: int32 [624, 256], P(('groups', 'ra'), 'dec'), parts along dimension 0, may hold values from 0 to 1, as said below
Outputs:
- smoothed: bfloat16 [512, 312, 256], P(('groups', 'band'), 'ra', 'dec'), parts along dimension 0
- channel_mean: float32 [512], P(('groups', 'band')), parts along dimension 0
- covariance: float32 [512, 256], P('groups', 'band'), parts along dimension 0
There are 2 independent parts, one for each index of `groups`. A program takes and returns all parts, laid end to end along the dimension named above; each array names one. Nothing has to cross between parts.
Inputs may be any that keep to these rules, and one draw needn't show every extreme that they name: `radii`: some channel has half-width exactly 17. 1 marks a pixel that enters the statistics; the pixel with declination index 0 is valid in every row.
All inputs are finite; a program needn't handle non-finite values.
Results may differ from a plain program's by a relative error of at most 0.012.
The roundings to bfloat16 on the way count: a program that leaves them out, or rounds other values in their place, can miss the bound.
Values may be sent and summed in bfloat16 or wider, within the bound.
A program may use at most 64 MiB of HBM per device.

v0:
```python
import jax
import jax.numpy as jnp
from jax import lax
from jax.sharding import PartitionSpec as P

RMAX = 17


def extended(array, sides, width, wrap):
    for axis, dim in sides:
        peers, length = (lax.axis_size(axis), array.shape[dim])
        up = [(i, (i + 1) % peers) for i in range(peers if wrap else peers - 1)]
        down = [(j, i) for i, j in up]
        last = lax.slice_in_dim(array, length - width, length, axis=dim)
        initial = lax.slice_in_dim(array, 0, width, axis=dim)
        before = lax.ppermute(last, axis, up)
        after = lax.ppermute(initial, axis, down)
        array = jnp.concatenate([before, array, after], axis=dim)
    return array


def beam_taps(radii, offsets):
    radius = radii.astype(jnp.float32)
    lead_shape = (radii.shape[0],) + (1,) * offsets.ndim
    radius = radius.reshape(lead_shape)
    spread = 0.5 * radius
    inside = jnp.abs(offsets)[None] <= radius
    return jnp.where(inside, jnp.exp(-(offsets * offsets)[None] / (2.0 * spread * spread)), 0.0)


def banded(radii, inner_count, outer_count):
    raw_taps = beam_taps(radii, jnp.arange(-RMAX, RMAX + 1).astype(jnp.float32))
    tap_total = jnp.sum(raw_taps, axis=1)
    offsets = (
        lax.broadcasted_iota(jnp.int32, (inner_count, outer_count), 0)
        - lax.broadcasted_iota(jnp.int32, (inner_count, outer_count), 1)
        - RMAX
    ).astype(jnp.float32)
    return (beam_taps(radii, offsets) / tap_total[:, None, None]).astype(jnp.bfloat16)


def local_sums(maps, mask_values):
    flat = maps.reshape(maps.shape[0], -1)
    weights = mask_values.reshape(-1)
    masked = flat * weights.astype(jnp.bfloat16)[None]
    sums = jnp.sum(masked.astype(jnp.float32), axis=1)
    return (masked, sums, jnp.sum(weights))


def per_device(sky_maps, radii, valid):
    channel_count, pixel_rows, pixel_cols = sky_maps.shape
    dec_band = banded(radii, pixel_cols + 2 * RMAX, pixel_cols)
    ra_band = banded(radii, pixel_rows + 2 * RMAX, pixel_rows)
    wrapped = extended(sky_maps, (("ra", 1),), RMAX, True)
    framed = extended(wrapped, (("dec", 2),), RMAX, False)
    across = jnp.einsum(
        "cxz,czy->cxy", framed, dec_band, preferred_element_type=jnp.float32
    ).astype(jnp.bfloat16)
    smoothed = jnp.einsum(
        "czy,czw->cwy", across, ra_band, preferred_element_type=jnp.float32
    ).astype(jnp.bfloat16)
    mask_values = valid.astype(jnp.float32)
    first_channel = lax.axis_index("band") * channel_count
    every = lax.all_gather(smoothed, "band", axis=0, tiled=True)
    masked, sums, count = local_sums(every, mask_values)
    own_rows = lax.dynamic_slice_in_dim(masked, first_channel, channel_count, 0)
    block = lax.dot_general(
        masked, own_rows, (((1,), (1,)), ((), ())), preferred_element_type=jnp.float32
    )
    sums, count, block = lax.psum((sums, count, block), ("ra", "dec"))
    mean_all = sums / count
    channel_mean = lax.dynamic_slice_in_dim(mean_all, first_channel, channel_count, 0)
    covariance = (block - count * mean_all[:, None] * channel_mean[None, :]) / (count - 1.0)
    return (smoothed, channel_mean, covariance)


def solution(mesh):
    return jax.shard_map(
        per_device,
        mesh=mesh,
        in_specs=(
            P(("groups", "band"), "ra", "dec"),
            P(("groups", "band")),
            P(("groups", "ra"), "dec"),
        ),
        out_specs=(P(("groups", "band"), "ra", "dec"), P(("groups", "band")), P("groups", "band")),
        check_vma=False,
    )
```

profile of v0, /device:TPU:0, one launch (start us, length us, event | category | flops | bytes accessed | tf_op | source)
XLA Modules:
  0.0 190.9 jit_solution(9157227778549513392)
XLA Ops:
  7.2 0.0 all-gather.2.cloned.1.call-start
  7.2 1.3 fusion.54
  8.5 3.1 %collective-permute-start = (bf16[128,17,128]{2,0,1:T(8,128)(2,1)S(1)}, bf16[128,17,128]{2,0,1:T(8,128)(2,1)S(1)}, u32[]{:S(2)}, u32[]{:S(2)}) collective-permute-start(bf16[128,17,128]{2,0,1:T(8,128)(2,1)S(1)} %get-tuple-element.24), channel_id=1, source_target_pairs={{0,4},{4,8},{8,12},{12,0},{1,5},{5,9},{9,13},{13,1},{2,6},{6,10},{... | collective-permute-start | bytes 1671176 | tf_op jit(solution)/shard_map/ppermute | solution.py:16
  11.6 2.1 %collective-permute-start.1 = (bf16[128,17,128]{2,0,1:T(8,128)(2,1)S(1)}, bf16[128,17,128]{2,0,1:T(8,128)(2,1)S(1)}, u32[]{:S(2)}, u32[]{:S(2)}) collective-permute-start(bf16[128,17,128]{2,0,1:T(8,128)(2,1)S(1)} %get-tuple-element.25), channel_id=1, source_target_pairs={{4,0},{8,4},{12,8},{0,12},{5,1},{9,5},{13,9},{1,13},{6,2},{10,6},{... | collective-permute-start | bytes 1671176 | tf_op jit(solution)/shard_map/ppermute | solution.py:17
  13.7 6.1 %copy.30 = bf16[128,78,128]{1,2,0:T(8,128)(2,1)} copy(bf16[128,78,128]{2,0,1:T(8,128)(2,1)} %param.3) | data formatting | bytes 5111808 | tf_op args[0]
  19.8 0.6 multiply_negate_fusion.1
  20.5 6.7 %collective-permute-done = bf16[128,17,128]{2,0,1:T(8,128)(2,1)S(1)} collective-permute-done((bf16[128,17,128]{2,0,1:T(8,128)(2,1)S(1)}, bf16[128,17,128]{2,0,1:T(8,128)(2,1)S(1)}, u32[]{:S(2)}, u32[]{:S(2)}) %collective-permute-start) | collective-permute-done | bytes 557088 | tf_op jit(solution)/shard_map/ppermute | solution.py:16
  27.1 3.3 %copy.29 = bf16[128,17,128]{1,2,0:T(8,128)(2,1)} copy(bf16[128,17,128]{2,0,1:T(8,128)(2,1)S(1)} %collective-permute-done) | data formatting | bytes 1114112 | tf_op jit(solution)/shard_map/ppermute | solution.py:16
  30.4 7.2 %collective-permute-done.1 = bf16[128,17,128]{2,0,1:T(8,128)(2,1)S(1)} collective-permute-done((bf16[128,17,128]{2,0,1:T(8,128)(2,1)S(1)}, bf16[128,17,128]{2,0,1:T(8,128)(2,1)S(1)}, u32[]{:S(2)}, u32[]{:S(2)}) %collective-permute-start.1) | collective-permute-done | bytes 557088 | tf_op jit(solution)/shard_map/ppermute | solution.py:17
  37.6 3.3 %copy.31 = bf16[128,17,128]{1,2,0:T(8,128)(2,1)} copy(bf16[128,17,128]{2,0,1:T(8,128)(2,1)S(1)} %collective-permute-done.1) | data formatting | bytes 1114112 | tf_op jit(solution)/shard_map/ppermute | solution.py:17
  40.9 0.0 copy-start.2
  40.9 4.2 %pad_maximum_fusion.2 = (bf16[128,112,17]{1,2,0:T(8,128)(2,1)S(1)}, bf16[128,112,17]{1,2,0:T(8,128)(2,1)S(1)}) fusion(bf16[128,17,128]{1,2,0:T(8,128)(2,1)} %copy.31, bf16[128,78,128]{1,2,0:T(8,128)(2,1)} %copy.30, bf16[128,17,128]{1,2,0:T(8,128)(2,1)} %copy.29), kind=kLoop, calls=%fused_computation.39 | loop fusion | flops 2924544 | bytes 4644864 | tf_op jit(solution)/shard_map/slice | solution.py:14
  45.1 0.5 copy.32
  45.5 3.4 %collective-permute-start.2 = (bf16[128,112,17]{0,1,2:T(8,128)(2,1)S(1)}, bf16[128,112,17]{0,1,2:T(8,128)(2,1)S(1)}, u32[]{:S(2)}, u32[]{:S(2)}) collective-permute-start(bf16[128,112,17]{0,1,2:T(8,128)(2,1)S(1)} %copy.32), channel_id=1, source_target_pairs={{0,2},{1,3},{4,6},{5,7},{8,10},{9,11},{12,14},{13,15},{16,18},{17,... | collective-permute-start | bytes 1462280 | tf_op jit(solution)/shard_map/ppermute | solution.py:16
  49.0 0.5 copy.33
  49.4 1.3 collective-permute-start.3
  50.8 0.0 copy-done.2
  50.8 0.1 fusion.48
  50.9 0.7 multiply_negate_fusion
  51.5 7.3 %collective-permute-done.2 = bf16[128,112,17]{0,1,2:T(8,128)(2,1)S(1)} collective-permute-done((bf16[128,112,17]{0,1,2:T(8,128)(2,1)S(1)}, bf16[128,112,17]{0,1,2:T(8,128)(2,1)S(1)}, u32[]{:S(2)}, u32[]{:S(2)}) %collective-permute-start.2) | collective-permute-done | bytes 487456 | tf_op jit(solution)/shard_map/ppermute | solution.py:16
  58.9 0.4 copy.34
  59.3 4.2 %collective-permute-done.3 = bf16[128,112,17]{0,1,2:T(8,128)(2,1)S(1)} collective-permute-done((bf16[128,112,17]{0,1,2:T(8,128)(2,1)S(1)}, bf16[128,112,17]{0,1,2:T(8,128)(2,1)S(1)}, u32[]{:S(2)}, u32[]{:S(2)}) %collective-permute-start.3) | collective-permute-done | bytes 487456 | tf_op jit(solution)/shard_map/ppermute | solution.py:17
  63.5 1.2 copy.35
  64.7 13.9 %fusion.34 = bf16[128,78,128]{2,1,0:T(8,128)(2,1)S(1)} fusion(f32[128]{0:T(128)S(1)} %fusion.48, f32[128]{0:T(128)S(1)} %multiply_multiply_fusion, f32[112,78]{0,1:T(8,128)S(1)} %get-tuple-element.30, f32[112,78]{0,1:T(8,128)} %get-tuple-element.31, f32[128]{0:T(128)S(1)} %convert_element_type.74, bf16[128,112,17]{1,2,0:T(8,128)(2,1)} %copy.35, ...), kind=kOutput, calls=%fused_computation.36 | convolution fusion | flops 926003200 | bytes 7438080 | tf_op jit(solution)/shard_map/czy,czw->cwy/dot_general | solution.py:59
  78.7 0.0 copy-start
  78.7 2.1 %copy.38 = bf16[128,78,128]{2,0,1:T(8,128)(2,1)} copy(bf16[128,78,128]{2,1,0:T(8,128)(2,1)S(1)} %fusion.34) | data formatting | bytes 5111808
  80.8 0.0 all-gather.2.cloned.1.call-update
  80.9 0.2 all-reduce.3.cloned.1.call-start
  81.1 0.0 copy-done
  81.1 0.6 convert_reduce_fusion.1
  81.7 13.3 %all-gather.2.cloned.1.call-done = bf16[256,78,128]{2,0,1:T(8,128)(2,1)} async-done(((bf16[128,78,128]{2,0,1:T(8,128)(2,1)}), bf16[256,78,128]{2,0,1:T(8,128)(2,1)}) %all-gather.2.cloned.1.call-update) | async-done | bytes 5111824 | tf_op jit(solution)/shard_map/all_gather | solution.py:64
  95.0 7.7 %copy.37 = bf16[256,78,128]{0,2,1:T(8,128)(2,1)} copy(bf16[256,78,128]{2,0,1:T(8,128)(2,1)} %all-gather.2.cloned.1.call-done) | data formatting | bytes 10223616 | tf_op jit(solution)/shard_map/all_gather | solution.py:64
  102.8 6.3 %bitcast_multiply_fusion = bf16[256,9984]{0,1:T(8,128)(2,1)S(1)} fusion(bf16[256,78,128]{0,2,1:T(8,128)(2,1)} %copy.37, bf16[9984]{0:T(1024)(128)(2,1)S(1)} %fusion.56), kind=kLoop, calls=%fused_computation.25 | loop fusion | flops 2555904 | bytes 10243584 | tf_op jit(solution)/shard_map/mul | solution.py:45
  109.0 2.3 %fusion.32 = f32[256,128]{1,0:T(8,128)} fusion(bf16[256,9984]{0,1:T(8,128)(2,1)S(1)} %bitcast_multiply_fusion, s32[]{:T(128)S(6)} %select_n.20), kind=kOutput, calls=%fused_computation.34 | convolution fusion | flops 654311424 | bytes 7798788 | tf_op jit(solution)/shard_map/dot_general | solution.py:67
  111.3 0.0 all-reduce.3.cloned.1.call-update
  111.3 3.7 %convert_reduce_fusion = f32[256]{0:T(256)S(1)} fusion(bf16[256,78,128]{2,0,1:T(8,128)(2,1)} %all-gather.2.cloned.1.call-done, bf16[78,128]{1,0:T(8,128)(2,1)S(1)} %convert_convert_fusion), kind=kLoop, calls=%fused_computation.4 | loop fusion | flops 7667456 | bytes 5132800 | tf_op jit(solution)/shard_map/reduce_sum | solution.py:46
  115.0 22.4 %all-reduce = (f32[256]{0:T(256)S(1)}, f32[]{:T(128)}) all-reduce(f32[256]{0:T(256)S(1)} %convert_reduce_fusion, f32[]{:T(128)} %convert_reduce_fusion.1), channel_id=1, replica_groups=mesh['groups'=2,'ra'=4,'dec'=2,'band'=2] {'ra','dec'}, use_global_device_ids=true, to_apply=%region_2.3 | all-reduce | flops 257 | bytes 2056 | tf_op jit(solution)/shard_map/psum | solution.py:70
  137.4 0.6 broadcast_multiply_fusion
  137.9 0.1 dynamic_slice.6
  138.0 0.0 copy-start.1
  138.6 43.8 %all-reduce.3.cloned.1.call-done = f32[256,128]{1,0:T(8,128)} async-done(((f32[256,128]{1,0:T(8,128)}), f32[256,128]{1,0:T(8,128)}) %all-reduce.3.cloned.1.call-update) | async-done | bytes 131088 | tf_op jit(solution)/shard_map/psum | solution.py:70
  182.3 1.7 subtract_divide_fusion
  184.0 0.0 copy-done.1
  (5 shorter events, 0.0 us)
Async XLA Ops:
  7.2 87.9 %all-gather.2.cloned.1.call-start = ((), (), s32[]{:S(2)}) async-start(), calls=%async_computation | async-start | bytes 7667712 | tf_op jit(solution)/shard_map/all_gather | solution.py:64
  8.5 18.6 %collective-permute-start = (bf16[128,17,128]{2,0,1:T(8,128)(2,1)S(1)}, bf16[128,17,128]{2,0,1:T(8,128)(2,1)S(1)}, u32[]{:S(2)}, u32[]{:S(2)}) collective-permute-start(bf16[128,17,128]{2,0,1:T(8,128)(2,1)S(1)} %get-tuple-element.24), channel_id=1, source_target_pairs={{0,4},{4,8},{8,12},{12,0},{1,5},{5,9},{9,13},{13,1},{2,6},{6,10},{... | collective-permute-start | bytes 1671176 | tf_op jit(solution)/shard_map/ppermute | solution.py:16
  11.6 26.0 %collective-permute-start.1 = (bf16[128,17,128]{2,0,1:T(8,128)(2,1)S(1)}, bf16[128,17,128]{2,0,1:T(8,128)(2,1)S(1)}, u32[]{:S(2)}, u32[]{:S(2)}) collective-permute-start(bf16[128,17,128]{2,0,1:T(8,128)(2,1)S(1)} %get-tuple-element.25), channel_id=1, source_target_pairs={{4,0},{8,4},{12,8},{0,12},{5,1},{9,5},{13,9},{1,13},{6,2},{10,6},{... | collective-permute-start | bytes 1671176 | tf_op jit(solution)/shard_map/ppermute | solution.py:17
  40.9 9.9 %copy-start.2 = (s32[128]{0:T(128)S(1)}, s32[128]{0:T(128)}, u32[]{:S(2)}) copy-start(s32[128]{0:T(128)} %param.4) | copy-start | bytes 1540
  45.5 13.3 %collective-permute-start.2 = (bf16[128,112,17]{0,1,2:T(8,128)(2,1)S(1)}, bf16[128,112,17]{0,1,2:T(8,128)(2,1)S(1)}, u32[]{:S(2)}, u32[]{:S(2)}) collective-permute-start(bf16[128,112,17]{0,1,2:T(8,128)(2,1)S(1)} %copy.32), channel_id=1, source_target_pairs={{0,2},{1,3},{4,6},{5,7},{8,10},{9,11},{12,14},{13,15},{16,18},{17,... | collective-permute-start | bytes 1462280 | tf_op jit(solution)/shard_map/ppermute | solution.py:16
  49.4 14.0 %collective-permute-start.3 = (bf16[128,112,17]{0,1,2:T(8,128)(2,1)S(1)}, bf16[128,112,17]{0,1,2:T(8,128)(2,1)S(1)}, u32[]{:S(2)}, u32[]{:S(2)}) collective-permute-start(bf16[128,112,17]{0,1,2:T(8,128)(2,1)S(1)} %copy.33), channel_id=1, source_target_pairs={{2,0},{3,1},{6,4},{7,5},{10,8},{11,9},{14,12},{15,13},{18,16},{19,... | collective-permute-start | bytes 1462280 | tf_op jit(solution)/shard_map/ppermute | solution.py:17
  78.7 2.4 %copy-start = (s32[78,128]{1,0:T(8,128)S(1)}, s32[78,128]{1,0:T(8,128)}, u32[]{:S(2)}) copy-start(s32[78,128]{1,0:T(8,128)} %param.5) | copy-start | bytes 119812
  80.9 101.5 %all-reduce.3.cloned.1.call-start = ((), (), s32[]{:S(2)}) async-start(), calls=%async_computation.1 | async-start | bytes 262144 | tf_op jit(solution)/shard_map/psum | solution.py:70
  138.0 46.0 %copy-start.1 = (f32[128]{0:T(128)}, f32[128]{0:T(128)S(1)}, u32[]{:S(2)}) copy-start(f32[128]{0:T(128)S(1)} %dynamic_slice.6) | copy-start | bytes 1540
Sparse Core Ops, SparseCore 0:
  81.0 13.9 all-gather.1
  111.4 70.8 all-reduce.2
where the time goes:
time: 191 us
  waiting for transfers between devices  82.4 us (43%)
  local copies, waits for them, and re-layouts  26.6 us (14%)
  blocking collectives  22.4 us (12%)
  other arithmetic  18.3 us (10%)
  matrix products  16.2 us (8%)
  between operations  14.7 us (8%)
  starting transfers between devices  10.1 us (5%)
    psum x1, waiting for transfers between devices, per_device(): sums, count, block = lax.psum((sums, count, block), ('ra', 'dec'))  43.8 us
    psum x1, blocking collectives, per_device(): sums, count, block = lax.psum((sums, count, block), ('ra', 'dec'))  22.4 us
    ppermute x2, waiting for transfers between devices, extended(): before = lax.ppermute(last, axis, up)  14 us
    dot_general x1, matrix products, per_device(): jnp.einsum('czy,czw->cwy', across, ra_band, preferred_element_type=jnp.fl...  13.9 us
    all_gather x1, waiting for transfers between devices, per_device(): every = lax.all_gather(smoothed, 'band', axis=0, tiled=True)  13.3 us
    ppermute x2, waiting for transfers between devices, extended(): after = lax.ppermute(initial, axis, down)  11.4 us
    unnamed x8, local copies, waits for them, and re-layouts  8.3 us
    all_gather x1, local copies, waits for them, and re-layouts, per_device(): every = lax.all_gather(smoothed, 'band', axis=0, tiled=True)  7.73 us
  transfers between devices with their start and end apart: 6, of which 6 were waited for; matrix products, arithmetic and copies ran while one was open for 9% of the time, Pallas kernels for 0%

commit v1 on v0

--- a/solution.py
+++ b/solution.py
@@ -67,7 +67,13 @@
     block = lax.dot_general(
         masked, own_rows, (((1,), (1,)), ((), ())), preferred_element_type=jnp.float32
     )
-    sums, count, block = lax.psum((sums, count, block), ("ra", "dec"))
+
+    def deliver_the_run(point, link_axis, which_axis="ra"):
+        for kk in (link_axis, which_axis):
+            point = lax.psum(point, axis_name=kk)
+        return point
+
+    sums, count, block = deliver_the_run((sums, count, block), "dec")
     mean_all = sums / count
     channel_mean = lax.dynamic_slice_in_dim(mean_all, first_channel, channel_count, 0)
     covariance = (block - count * mean_all[:, None] * channel_mean[None, :]) / (count - 1.0)

time: 191 us -> 180 us (0.942)
  waiting for transfers between devices: 82.4 us -> 75 us
  blocking collectives: 22.4 us -> 18.2 us
    psum x1 -> x2, waiting for transfers between devices: 43.8 us -> 36.4 us  [deliver_the_run(): point = lax.psum(point, axis_name=kk)]
    psum x1 -> x2, blocking collectives: 22.4 us -> 18.2 us  [deliver_the_run(): point = lax.psum(point, axis_name=kk)]
  transfers between devices with their start and end apart: 6 -> 7, of which waited for: 6 -> 7; matrix products, arithmetic and copies ran while one was open for 9% -> 9% of each run, Pallas kernels for 0% -> 0%
where the time goes in v1:
time: 180 us; the launch traced here: 179 us
  waiting for transfers between devices  75 us (42%)
  local copies, waits for them, and re-layouts  26.6 us (15%)
  other arithmetic  18.4 us (10%)
  blocking collectives  18.2 us (10%)
  matrix products  16.2 us (9%)
  between operations  14.5 us (8%)
  starting transfers between devices  10.2 us (6%)
    psum x2, waiting for transfers between devices, deliver_the_run(): point = lax.psum(point, axis_name=kk)  36.4 us
    psum x2, blocking collectives, deliver_the_run(): point = lax.psum(point, axis_name=kk)  18.2 us
    ppermute x2, waiting for transfers between devices, extended(): before = lax.ppermute(last, axis, up)  14 us
    dot_general x1, matrix products, per_device(): jnp.einsum('czy,czw->cwy', across, ra_band, preferred_element_type=jnp.fl...  13.9 us
    all_gather x1, waiting for transfers between devices, per_device(): every = lax.all_gather(smoothed, 'band', axis=0, tiled=True)  13.3 us
    ppermute x2, waiting for transfers between devices, extended(): after = lax.ppermute(initial, axis, down)  11.4 us
    unnamed x8, local copies, waits for them, and re-layouts  8.3 us
    all_gather x1, local copies, waits for them, and re-layouts, per_device(): every = lax.all_gather(smoothed, 'band', axis=0, tiled=True)  7.74 us
  transfers between devices with their start and end apart: 7, of which 7 were waited for; matrix products, arithmetic and copies ran while one was open for 9% of the time, Pallas kernels for 0%

profile of v1, /device:TPU:0, one launch (start us, length us, event | category | flops | bytes accessed | tf_op | source)
XLA Modules:
  0.0 179.2 jit_solution(224410944097852753)
XLA Ops:
  7.2 0.0 all-gather.2.cloned.1.call-start
  7.2 1.3 fusion.54
  8.5 3.1 %collective-permute-start = (bf16[128,17,128]{2,0,1:T(8,128)(2,1)S(1)}, bf16[128,17,128]{2,0,1:T(8,128)(2,1)S(1)}, u32[]{:S(2)}, u32[]{:S(2)}) collective-permute-start(bf16[128,17,128]{2,0,1:T(8,128)(2,1)S(1)} %get-tuple-element.26), channel_id=1, source_target_pairs={{0,4},{4,8},{8,12},{12,0},{1,5},{5,9},{9,13},{13,1},{2,6},{6,10},{... | collective-permute-start | bytes 1671176 | tf_op jit(solution)/shard_map/ppermute | solution.py:16
  11.6 2.1 %collective-permute-start.1 = (bf16[128,17,128]{2,0,1:T(8,128)(2,1)S(1)}, bf16[128,17,128]{2,0,1:T(8,128)(2,1)S(1)}, u32[]{:S(2)}, u32[]{:S(2)}) collective-permute-start(bf16[128,17,128]{2,0,1:T(8,128)(2,1)S(1)} %get-tuple-element.27), channel_id=1, source_target_pairs={{4,0},{8,4},{12,8},{0,12},{5,1},{9,5},{13,9},{1,13},{6,2},{10,6},{... | collective-permute-start | bytes 1671176 | tf_op jit(solution)/shard_map/ppermute | solution.py:17
  13.7 6.2 %copy.30 = bf16[128,78,128]{1,2,0:T(8,128)(2,1)} copy(bf16[128,78,128]{2,0,1:T(8,128)(2,1)} %param.3) | data formatting | bytes 5111808 | tf_op args[0]
  19.8 0.6 multiply_negate_fusion.1
  20.5 6.6 %collective-permute-done = bf16[128,17,128]{2,0,1:T(8,128)(2,1)S(1)} collective-permute-done((bf16[128,17,128]{2,0,1:T(8,128)(2,1)S(1)}, bf16[128,17,128]{2,0,1:T(8,128)(2,1)S(1)}, u32[]{:S(2)}, u32[]{:S(2)}) %collective-permute-start) | collective-permute-done | bytes 557088 | tf_op jit(solution)/shard_map/ppermute | solution.py:16
  27.1 3.3 %copy.29 = bf16[128,17,128]{1,2,0:T(8,128)(2,1)} copy(bf16[128,17,128]{2,0,1:T(8,128)(2,1)S(1)} %collective-permute-done) | data formatting | bytes 1114112 | tf_op jit(solution)/shard_map/ppermute | solution.py:16
  30.4 7.2 %collective-permute-done.1 = bf16[128,17,128]{2,0,1:T(8,128)(2,1)S(1)} collective-permute-done((bf16[128,17,128]{2,0,1:T(8,128)(2,1)S(1)}, bf16[128,17,128]{2,0,1:T(8,128)(2,1)S(1)}, u32[]{:S(2)}, u32[]{:S(2)}) %collective-permute-start.1) | collective-permute-done | bytes 557088 | tf_op jit(solution)/shard_map/ppermute | solution.py:17
  37.6 3.3 %copy.31 = bf16[128,17,128]{1,2,0:T(8,128)(2,1)} copy(bf16[128,17,128]{2,0,1:T(8,128)(2,1)S(1)} %collective-permute-done.1) | data formatting | bytes 1114112 | tf_op jit(solution)/shard_map/ppermute | solution.py:17
  40.9 0.0 copy-start.2
  40.9 4.2 %pad_maximum_fusion.2 = (bf16[128,112,17]{1,2,0:T(8,128)(2,1)S(1)}, bf16[128,112,17]{1,2,0:T(8,128)(2,1)S(1)}) fusion(bf16[128,17,128]{1,2,0:T(8,128)(2,1)} %copy.31, bf16[128,78,128]{1,2,0:T(8,128)(2,1)} %copy.30, bf16[128,17,128]{1,2,0:T(8,128)(2,1)} %copy.29), kind=kLoop, calls=%fused_computation.39 | loop fusion | flops 2924544 | bytes 4644864 | tf_op jit(solution)/shard_map/slice | solution.py:14
  45.1 0.5 copy.32
  45.5 3.4 %collective-permute-start.2 = (bf16[128,112,17]{0,1,2:T(8,128)(2,1)S(1)}, bf16[128,112,17]{0,1,2:T(8,128)(2,1)S(1)}, u32[]{:S(2)}, u32[]{:S(2)}) collective-permute-start(bf16[128,112,17]{0,1,2:T(8,128)(2,1)S(1)} %copy.32), channel_id=1, source_target_pairs={{0,2},{1,3},{4,6},{5,7},{8,10},{9,11},{12,14},{13,15},{16,18},{17,... | collective-permute-start | bytes 1462280 | tf_op jit(solution)/shard_map/ppermute | solution.py:16
  49.0 0.5 copy.33
  49.4 1.3 collective-permute-start.3
  50.8 0.0 copy-done.2
  50.8 0.1 fusion.48
  50.9 0.7 multiply_negate_fusion
  51.5 7.3 %collective-permute-done.2 = bf16[128,112,17]{0,1,2:T(8,128)(2,1)S(1)} collective-permute-done((bf16[128,112,17]{0,1,2:T(8,128)(2,1)S(1)}, bf16[128,112,17]{0,1,2:T(8,128)(2,1)S(1)}, u32[]{:S(2)}, u32[]{:S(2)}) %collective-permute-start.2) | collective-permute-done | bytes 487456 | tf_op jit(solution)/shard_map/ppermute | solution.py:16
  58.9 0.4 copy.34
  59.3 4.2 %collective-permute-done.3 = bf16[128,112,17]{0,1,2:T(8,128)(2,1)S(1)} collective-permute-done((bf16[128,112,17]{0,1,2:T(8,128)(2,1)S(1)}, bf16[128,112,17]{0,1,2:T(8,128)(2,1)S(1)}, u32[]{:S(2)}, u32[]{:S(2)}) %collective-permute-start.3) | collective-permute-done | bytes 487456 | tf_op jit(solution)/shard_map/ppermute | solution.py:17
  63.5 1.2 copy.35
  64.7 13.9 %fusion.34 = bf16[128,78,128]{2,1,0:T(8,128)(2,1)S(1)} fusion(f32[128]{0:T(128)S(1)} %fusion.48, f32[128]{0:T(128)S(1)} %multiply_multiply_fusion, f32[112,78]{0,1:T(8,128)S(1)} %get-tuple-element.32, f32[112,78]{0,1:T(8,128)} %get-tuple-element.33, f32[128]{0:T(128)S(1)} %convert_element_type.74, bf16[128,112,17]{1,2,0:T(8,128)(2,1)} %copy.35, ...), kind=kOutput, calls=%fused_computation.36 | convolution fusion | flops 926003200 | bytes 7438080 | tf_op jit(solution)/shard_map/czy,czw->cwy/dot_general | solution.py:59
  78.7 0.0 copy-start
  78.7 2.1 %copy.38 = bf16[128,78,128]{2,0,1:T(8,128)(2,1)} copy(bf16[128,78,128]{2,1,0:T(8,128)(2,1)S(1)} %fusion.34) | data formatting | bytes 5111808
  80.8 0.0 all-gather.2.cloned.1.call-update
  80.9 0.2 all-reduce.5.cloned.1.call-start
  81.1 0.0 copy-done
  81.1 0.6 convert_reduce_fusion.1
  81.7 13.3 %all-gather.2.cloned.1.call-done = bf16[256,78,128]{2,0,1:T(8,128)(2,1)} async-done(((bf16[128,78,128]{2,0,1:T(8,128)(2,1)}), bf16[256,78,128]{2,0,1:T(8,128)(2,1)}) %all-gather.2.cloned.1.call-update) | async-done | bytes 5111824 | tf_op jit(solution)/shard_map/all_gather | solution.py:64
  95.0 7.7 %copy.37 = bf16[256,78,128]{0,2,1:T(8,128)(2,1)} copy(bf16[256,78,128]{2,0,1:T(8,128)(2,1)} %all-gather.2.cloned.1.call-done) | data formatting | bytes 10223616 | tf_op jit(solution)/shard_map/all_gather | solution.py:64
  102.8 6.3 %bitcast_multiply_fusion = bf16[256,9984]{0,1:T(8,128)(2,1)S(1)} fusion(bf16[256,78,128]{0,2,1:T(8,128)(2,1)} %copy.37, bf16[9984]{0:T(1024)(128)(2,1)S(1)} %fusion.56), kind=kLoop, calls=%fused_computation.25 | loop fusion | flops 2555904 | bytes 10243584 | tf_op jit(solution)/shard_map/mul | solution.py:45
  109.1 2.3 %fusion.32 = f32[256,128]{1,0:T(8,128)} fusion(bf16[256,9984]{0,1:T(8,128)(2,1)S(1)} %bitcast_multiply_fusion, s32[]{:T(128)S(6)} %select_n.20), kind=kOutput, calls=%fused_computation.34 | convolution fusion | flops 654311424 | bytes 7798788 | tf_op jit(solution)/shard_map/dot_general | solution.py:67
  111.3 0.0 all-reduce.5.cloned.1.call-update
  111.3 0.0 all-reduce.7.cloned.1.call-start
  111.4 3.7 %convert_reduce_fusion = f32[256]{0:T(256)S(1)} fusion(bf16[256,78,128]{2,0,1:T(8,128)(2,1)} %all-gather.2.cloned.1.call-done, bf16[78,128]{1,0:T(8,128)(2,1)S(1)} %convert_convert_fusion), kind=kLoop, calls=%fused_computation.4 | loop fusion | flops 7667456 | bytes 5132800 | tf_op jit(solution)/shard_map/reduce_sum | solution.py:46
  115.0 5.6 %all-reduce.1 = (f32[256]{0:T(256)S(1)}, f32[]{:T(128)}) all-reduce(f32[256]{0:T(256)S(1)} %convert_reduce_fusion, f32[]{:T(128)} %convert_reduce_fusion.1), channel_id=1, replica_groups=mesh['groups'=2,'ra'=4,'dec'=2,'band'=2] {'dec'}, use_global_device_ids=true, to_apply=%region_2.3 | all-reduce | flops 257 | bytes 2056 | tf_op jit(solution)/shard_map/psum | solution.py:73
  120.6 12.6 %all-reduce = (f32[256]{0:T(256)S(1)}, f32[]{:T(128)}) all-reduce(f32[256]{0:T(256)S(1)} %get-tuple-element.20, f32[]{:T(128)} %get-tuple-element.21), channel_id=1, replica_groups=mesh['groups'=2,'ra'=4,'dec'=2,'band'=2] {'ra'}, use_global_device_ids=true, to_apply=%region_3.4 | all-reduce | flops 257 | bytes 2056 | tf_op jit(solution)/shard_map/psum | solution.py:73
  133.3 0.9 all-reduce.5.cloned.1.call-done
  134.2 0.0 all-reduce.7.cloned.1.call-update
  134.2 0.6 broadcast_multiply_fusion
  134.8 0.1 dynamic_slice.6
  134.9 0.0 copy-start.1
  135.6 35.4 %all-reduce.7.cloned.1.call-done = f32[256,128]{1,0:T(8,128)} async-done(((f32[256,128]{1,0:T(8,128)}), f32[256,128]{1,0:T(8,128)}) %all-reduce.7.cloned.1.call-update) | async-done | bytes 131088 | tf_op jit(solution)/shard_map/psum | solution.py:73
  171.0 1.7 subtract_divide_fusion
  172.7 0.0 copy-done.1
  (5 shorter events, 0.0 us)
Async XLA Ops:
  7.2 87.9 %all-gather.2.cloned.1.call-start = ((), (), s32[]{:S(2)}) async-start(), calls=%async_computation | async-start | bytes 7667712 | tf_op jit(solution)/shard_map/all_gather | solution.py:64
  8.5 18.6 %collective-permute-start = (bf16[128,17,128]{2,0,1:T(8,128)(2,1)S(1)}, bf16[128,17,128]{2,0,1:T(8,128)(2,1)S(1)}, u32[]{:S(2)}, u32[]{:S(2)}) collective-permute-start(bf16[128,17,128]{2,0,1:T(8,128)(2,1)S(1)} %get-tuple-element.26), channel_id=1, source_target_pairs={{0,4},{4,8},{8,12},{12,0},{1,5},{5,9},{9,13},{13,1},{2,6},{6,10},{... | collective-permute-start | bytes 1671176 | tf_op jit(solution)/shard_map/ppermute | solution.py:16
  11.6 26.0 %collective-permute-start.1 = (bf16[128,17,128]{2,0,1:T(8,128)(2,1)S(1)}, bf16[128,17,128]{2,0,1:T(8,128)(2,1)S(1)}, u32[]{:S(2)}, u32[]{:S(2)}) collective-permute-start(bf16[128,17,128]{2,0,1:T(8,128)(2,1)S(1)} %get-tuple-element.27), channel_id=1, source_target_pairs={{4,0},{8,4},{12,8},{0,12},{5,1},{9,5},{13,9},{1,13},{6,2},{10,6},{... | collective-permute-start | bytes 1671176 | tf_op jit(solution)/shard_map/ppermute | solution.py:17
  40.9 9.9 %copy-start.2 = (s32[128]{0:T(128)S(1)}, s32[128]{0:T(128)}, u32[]{:S(2)}) copy-start(s32[128]{0:T(128)} %param.4) | copy-start | bytes 1540
  45.5 13.3 %collective-permute-start.2 = (bf16[128,112,17]{0,1,2:T(8,128)(2,1)S(1)}, bf16[128,112,17]{0,1,2:T(8,128)(2,1)S(1)}, u32[]{:S(2)}, u32[]{:S(2)}) collective-permute-start(bf16[128,112,17]{0,1,2:T(8,128)(2,1)S(1)} %copy.32), channel_id=1, source_target_pairs={{0,2},{1,3},{4,6},{5,7},{8,10},{9,11},{12,14},{13,15},{16,18},{17,... | collective-permute-start | bytes 1462280 | tf_op jit(solution)/shard_map/ppermute | solution.py:16
  49.4 14.0 %collective-permute-start.3 = (bf16[128,112,17]{0,1,2:T(8,128)(2,1)S(1)}, bf16[128,112,17]{0,1,2:T(8,128)(2,1)S(1)}, u32[]{:S(2)}, u32[]{:S(2)}) collective-permute-start(bf16[128,112,17]{0,1,2:T(8,128)(2,1)S(1)} %copy.33), channel_id=1, source_target_pairs={{2,0},{3,1},{6,4},{7,5},{10,8},{11,9},{14,12},{15,13},{18,16},{19,... | collective-permute-start | bytes 1462280 | tf_op jit(solution)/shard_map/ppermute | solution.py:17
  78.7 2.4 %copy-start = (s32[78,128]{1,0:T(8,128)S(1)}, s32[78,128]{1,0:T(8,128)}, u32[]{:S(2)}) copy-start(s32[78,128]{1,0:T(8,128)} %param.5) | copy-start | bytes 119812
  80.9 53.3 %all-reduce.5.cloned.1.call-start = ((), (), s32[]{:S(2)}) async-start(), calls=%async_computation.1 | async-start | bytes 262144 | tf_op jit(solution)/shard_map/psum | solution.py:73
  111.3 59.6 %all-reduce.7.cloned.1.call-start = ((), (), s32[]{:S(2)}) async-start(), calls=%async_computation.2 | async-start | bytes 262144 | tf_op jit(solution)/shard_map/psum | solution.py:73
  134.9 37.7 %copy-start.1 = (f32[128]{0:T(128)}, f32[128]{0:T(128)S(1)}, u32[]{:S(2)}) copy-start(f32[128]{0:T(128)S(1)} %dynamic_slice.6) | copy-start | bytes 1540
Sparse Core Ops, SparseCore 0:
  81.0 13.9 all-gather.1
  111.5 22.6 all-reduce.4
  136.5 34.4 all-reduce.6
